TPU v7x, 32 devices: a whole 2x2x4 slice. The times are simulated.
32 devices in a mesh: dp: 8 (over y, x, core), tensor: 4 (over z).
Axes of the slice: x: 2, y: 2, z: 4, core: 2. Of those that a mesh axis runs over, the one named last changes fastest.
Arguments:
- tokens: bfloat16 [8192, 1024], P(('dp', 'tensor')), may hold values from -6 to 6
- cotangent: bfloat16 [8192, 1024], P(('dp', 'tensor')), may hold values from -6 to 6
- norm_gain: float32 [1024], replicated, may hold values from 0.1 to 1.9
- w_gate: bfloat16 [1024, 2048], P('dp', 'tensor'), may hold values from -0.1875 to 0.1875
- w_value: bfloat16 [1024, 2048], P('dp', 'tensor'), may hold values from -0.1875 to 0.1875
- w_bc: bfloat16 [1024, 256], P('dp'), may hold values from -0.1875 to 0.1875
- w_step: bfloat16 [1024, 32], P('dp', 'tensor'), may hold values from -0.1875 to 0.1875
- conv_value: float32 [5, 2048], P(None, 'tensor'), may hold values from -3 to 3
- conv_bc: float32 [5, 256], replicated, may hold values from -3 to 3
- head_params: float32 [3, 32], P(None, 'tensor'), may hold values from -2 to 1
- gnorm_gain: float32 [2048], P('tensor'), may hold values from 0.1 to 1.9
- w_out: bfloat16 [2048, 1024], P('tensor', 'dp'), may hold values from -0.125 to 0.125
Outputs:
- block_out: float32 [8192, 1024], P(('dp', 'tensor'))
- grad_input: float32 [8192, 1024], P(('dp', 'tensor'))
- grad_norm_gain: float32 [1024], replicated
- grad_w_gate: float32 [1024, 2048], P('dp', 'tensor')
- grad_w_value: float32 [1024, 2048], P('dp', 'tensor')
- grad_w_bc: float32 [1024, 256], P('dp')
- grad_w_step: float32 [1024, 32], P('dp', 'tensor')
- grad_conv_value: float32 [5, 2048], P(None, 'tensor')
- grad_conv_bc: float32 [5, 256], replicated
- grad_head_params: float32 [3, 32], P(None, 'tensor')
- grad_gnorm_gain: float32 [2048], P('tensor')
- grad_w_out: float32 [2048, 1024], P('tensor', 'dp')
All inputs are finite; a program needn't handle non-finite values.
Results may differ from a plain program's by a relative error of at most 0.02.
Values may be sent and summed in bfloat16 or wider, within the bound.
A program may use at most 128 MiB of HBM per device.

v0:
```python
import jax
import jax.numpy as jnp
from jax import lax
from jax.sharding import PartitionSpec as P

D = 1024
HEADS = 32
SPAN = 256
SEQLEN = 1024
INNER = 2048
EPSILON = 1e-05
HIGHEST = lax.Precision.HIGHEST


def causal(sequence, taps):
    width = taps.shape[0] - 1
    padded = jnp.pad(sequence, ((width - 1, 0), (0, 0)))
    total = jnp.zeros_like(sequence) + taps[width]
    for offset in range(width):
        total = total + taps[offset] * padded[offset : offset + sequence.shape[0]]
    return total


def scan_state(values, step_size, rate, b_map, c_map):
    length, heads, hdim_local = values.shape
    count = length // SPAN
    values_c = values.reshape(count, SPAN, heads, hdim_local)
    step_c = step_size.reshape(count, SPAN, heads)
    b_c = b_map.reshape(count, SPAN, b_map.shape[1])
    c_c = c_map.reshape(count, SPAN, c_map.shape[1])
    lower = (
        lax.broadcasted_iota(jnp.int32, (SPAN, SPAN), 0)
        >= lax.broadcasted_iota(jnp.int32, (SPAN, SPAN), 1)
    )[None, :, :]

    def span_step(state, block):
        block_values, block_step, block_b, block_c = block
        logdecay = jnp.cumsum(block_step * rate[None, :], axis=0)
        heads_first = logdecay.T
        inner_prod = jnp.dot(
            block_c, block_b.T, precision=HIGHEST, preferred_element_type=jnp.float32
        )
        spacing = heads_first[:, :, None] - heads_first[:, None, :]
        kernel = jnp.where(lower, jnp.exp(jnp.where(lower, spacing, -60.0)), 0.0)
        kernel = kernel * inner_prod[None, :, :] * block_step.T[:, None, :]
        within = jnp.einsum("hij,jhp->ihp", kernel, block_values, precision=HIGHEST)
        carried = (
            jnp.einsum("in,hpn->ihp", block_c, state, precision=HIGHEST)
            * jnp.exp(logdecay)[:, :, None]
        )
        trailing = jnp.exp(logdecay[-1][None, :] - logdecay) * block_step
        update = jnp.einsum("jh,jhp,jn->hpn", trailing, block_values, block_b, precision=HIGHEST)
        new_state = state * jnp.exp(logdecay[-1])[:, None, None] + update
        return (new_state, within + carried)

    start = jnp.zeros((heads, hdim_local, b_map.shape[1]), jnp.float32)
    final_state, outputs = lax.scan(jax.checkpoint(span_step), start, (values_c, step_c, b_c, c_c))
    return outputs.reshape(length, heads, hdim_local)


def mixer(gate_pre, value_pre, shared_pre, step_pre, conv_value, conv_bc, head_params):
    length = gate_pre.shape[0]
    heads = step_pre.shape[1]
    values = jax.nn.silu(causal(value_pre, conv_value))
    shared = jax.nn.silu(causal(shared_pre, conv_bc))
    half_width = shared.shape[1] // 2
    step_size = jax.nn.softplus(step_pre + head_params[0])
    rate = -jnp.exp(head_params[1])
    headed = values.reshape(length, heads, -1)
    scanned = scan_state(headed, step_size, rate, shared[:, :half_width], shared[:, half_width:])
    scanned = scanned + head_params[2][None, :, None] * headed
    return scanned.reshape(length, -1) * jax.nn.silu(gate_pre)


def group_mix(gate_pre, value_pre, shared_pre, step_pre, conv_value, conv_bc, head_params):
    return jax.vmap(mixer, in_axes=(0, 0, 0, 0, None, None, None))(
        gate_pre, value_pre, shared_pre, step_pre, conv_value, conv_bc, head_params
    )


def project(normed, fetched):
    groups = normed.shape[0] // SEQLEN
    outputs = []
    for matrix in fetched[:4]:
        product = jnp.dot(normed, matrix, preferred_element_type=jnp.float32)
        outputs.append(product.reshape(groups, SEQLEN, -1))
    return outputs


def contract_rows(left, right):
    return lax.dot_general(
        left, right, (((0,), (0,)), ((), ())), preferred_element_type=jnp.float32
    )


def contract_cols(left, right):
    return lax.dot_general(
        left, right, (((1,), (1,)), ((), ())), preferred_element_type=jnp.float32
    )


def place(piece, total):
    start = lax.axis_index("tensor") * piece.shape[-1]
    filled = jnp.zeros(piece.shape[:-1] + (total,), jnp.float32)
    return lax.dynamic_update_slice_in_dim(filled, piece, start, piece.ndim - 1)


def pick(whole, width):
    start = lax.axis_index("tensor") * width
    return lax.dynamic_slice_in_dim(whole, start, width, whole.ndim - 1)


def body(
    tokens,
    cotangent,
    norm_gain,
    w_gate,
    w_value,
    w_bc,
    w_step,
    conv_value,
    conv_bc,
    head_params,
    gnorm_gain,
    w_out,
):
    rows32 = tokens.astype(jnp.float32)
    grad_out = cotangent.astype(jnp.float32)
    scaling = lax.rsqrt(jnp.mean(rows32 * rows32, axis=1, keepdims=True) + EPSILON)
    normed = lax.all_gather(
        (rows32 * scaling * norm_gain).astype(jnp.bfloat16), "tensor", axis=0, tiled=True
    )
    fetched = (
        lax.all_gather(w_gate, "dp", axis=0, tiled=True),
        lax.all_gather(w_value, "dp", axis=0, tiled=True),
        lax.all_gather(w_bc, "dp", axis=0, tiled=True),
        lax.all_gather(w_step, "dp", axis=0, tiled=True),
        lax.all_gather(w_out, "dp", axis=1, tiled=True),
    )
    projected = project(normed, fetched)
    mixed_in, mix_back = jax.vjp(
        group_mix,
        projected[0],
        projected[1],
        projected[2],
        projected[3],
        conv_value,
        conv_bc,
        head_params,
    )
    group_rows = normed.shape[0]
    gated = mixed_in.reshape(group_rows, -1)
    total_sq = lax.psum(jnp.sum(gated * gated, axis=1), "tensor")
    rescale = lax.rsqrt(total_sq / INNER + EPSILON)[:, None]
    unitized = gated * rescale
    scaled = (unitized * gnorm_gain).astype(jnp.bfloat16)
    branch = jnp.dot(scaled, fetched[4], preferred_element_type=jnp.float32)
    block_out = rows32 + lax.psum_scatter(
        branch.astype(jnp.bfloat16), "tensor", scatter_dimension=0, tiled=True
    ).astype(jnp.float32)
    grad_rows = lax.all_gather(cotangent, "tensor", axis=0, tiled=True)
    grad_scaled = contract_cols(grad_rows, fetched[4])
    grad_w_out = contract_rows(scaled, grad_rows)
    grad_gnorm_full = place(jnp.sum(grad_scaled * unitized, axis=0), INNER)
    grad_unit = grad_scaled * gnorm_gain
    cross_sum = lax.psum(jnp.sum(grad_unit * gated, axis=1), "tensor")
    grad_gated = (
        rescale * grad_unit - gated * (rescale * rescale * rescale) * cross_sum[:, None] / INNER
    )
    mix_grads = mix_back(grad_gated.reshape(mixed_in.shape))
    grad_normed = jnp.zeros((group_rows, normed.shape[1]), jnp.float32)
    weight_terms = []
    for index in range(4):
        rounded = mix_grads[index].reshape(group_rows, -1).astype(jnp.bfloat16)
        grad_normed = grad_normed + contract_cols(rounded, fetched[index])
        weight_terms.append(contract_rows(normed, rounded))
    grad_h = lax.psum_scatter(
        grad_normed.astype(jnp.bfloat16), "tensor", scatter_dimension=0, tiled=True
    ).astype(jnp.float32)
    scaled_grad = grad_h * norm_gain
    grad_input = (
        grad_out
        + scaling * scaled_grad
        - rows32
        * (scaling * scaling * scaling)
        * jnp.sum(scaled_grad * rows32, axis=1, keepdims=True)
        / D
    )
    grad_norm_local = jnp.sum(grad_h * rows32 * scaling, axis=0)
    summed = (
        lax.psum_scatter(
            weight_terms[0].astype(jnp.bfloat16), "dp", scatter_dimension=0, tiled=True
        ).astype(jnp.float32),
        lax.psum_scatter(
            weight_terms[1].astype(jnp.bfloat16), "dp", scatter_dimension=0, tiled=True
        ).astype(jnp.float32),
        lax.psum_scatter(
            weight_terms[2].astype(jnp.bfloat16), "dp", scatter_dimension=0, tiled=True
        ).astype(jnp.float32),
        lax.psum_scatter(
            weight_terms[3].astype(jnp.bfloat16), "dp", scatter_dimension=0, tiled=True
        ).astype(jnp.float32),
        lax.psum_scatter(
            grad_w_out.astype(jnp.bfloat16), "dp", scatter_dimension=1, tiled=True
        ).astype(jnp.float32),
    )
    grad_w_bc = lax.psum(summed[2].astype(jnp.bfloat16), "tensor").astype(jnp.float32)
    conv_cols = mix_grads[4].shape[1]
    head_cols = mix_grads[6].shape[1]
    small = lax.psum(
        (
            place(mix_grads[4], INNER),
            place(mix_grads[6], HEADS),
            grad_gnorm_full,
            mix_grads[5],
            grad_norm_local,
        ),
        ("dp", "tensor"),
    )
    grad_conv_value = pick(small[0], conv_cols)
    grad_head_params = pick(small[1], head_cols)
    grad_gnorm_gain = pick(small[2], conv_cols)
    return (
        block_out,
        grad_input,
        small[4],
        summed[0],
        summed[1],
        grad_w_bc,
        summed[3],
        grad_conv_value,
        small[3],
        grad_head_params,
        grad_gnorm_gain,
        summed[4],
    )


def solution(mesh):
    in_specs = (
        P(("dp", "tensor"), None),
        P(("dp", "tensor"), None),
        P(),
        P("dp", "tensor"),
        P("dp", "tensor"),
        P("dp", None),
        P("dp", "tensor"),
        P(None, "tensor"),
        P(),
        P(None, "tensor"),
        P("tensor"),
        P("tensor", "dp"),
    )
    out_specs = (
        P(("dp", "tensor"), None),
        P(("dp", "tensor"), None),
        P(),
        P("dp", "tensor"),
        P("dp", "tensor"),
        P("dp", None),
        P("dp", "tensor"),
        P(None, "tensor"),
        P(),
        P(None, "tensor"),
        P("tensor"),
        P("tensor", "dp"),
    )
    return jax.shard_map(body, mesh=mesh, in_specs=in_specs, out_specs=out_specs, check_vma=False)
```

profile of v0, /device:TPU:10, one launch (start us, length us, event | category | flops | bytes accessed | tf_op | source)
XLA Modules:
  0.0 658.2 jit_solution(18267086036678611181)
XLA Ops:
  16.0 8.9 %all_gather.22 = bf16[1024,8]{0,1:T(8,128)(2,1)S(1)} all-gather(bf16[128,8]{0,1:T(8,128)(2,1)S(1)} %copy-done.59), channel_id=1, replica_groups=mesh['dp'=8,'tensor'=4] {'dp'}, dimensions={0}, use_global_device_ids=true | all-gather | bytes 18432 | tf_op jit(solution)/shard_map/all_gather | solution.py:137
  24.9 8.9 %all_gather.24 = bf16[1024,256]{1,0:T(8,128)(2,1)S(1)} all-gather(bf16[128,256]{1,0:T(8,128)(2,1)S(1)} %copy-done.23), channel_id=1, replica_groups=mesh['dp'=8,'tensor'=4] {'dp'}, dimensions={0}, use_global_device_ids=true | all-gather | bytes 589824 | tf_op jit(solution)/shard_map/all_gather | solution.py:136
  33.8 23.6 %all-gather.6.cloned.1.call-done = bf16[1024,1024]{1,0:T(8,128)(2,1)} async-done(((bf16[256,1024]{1,0:T(8,128)(2,1)}), bf16[1024,1024]{1,0:T(8,128)(2,1)}) %all-gather.6.cloned.1.call-update) | async-done | bytes 2097168 | tf_op jit(solution)/shard_map/all_gather | solution.py:130
  62.4 20.7 %all-gather.8.cloned.1.call-done = bf16[1024,512]{1,0:T(8,128)(2,1)} async-done(((bf16[128,512]{1,0:T(8,128)(2,1)}), bf16[1024,512]{1,0:T(8,128)(2,1)}) %all-gather.8.cloned.1.call-update) | async-done | bytes 1048592 | tf_op jit(solution)/shard_map/all_gather | solution.py:135
  85.6 2.7 fusion.137
  88.3 5.1 reshape.1137
  93.4 3.8 copy.149
  97.2 2.9 compare_select_fusion.2
  101.7 44.2 %while.44 = (s32[]{:T(128)}, f32[1,8,64,128]{3,2,1,0:T(8,128)S(1)}, f32[4,1,256,8,64]{2,4,3,1,0:T(8,128)}, f32[4,1,8,64,128]{4,3,2,1,0:T(8,128)}, f32[4,1,256,8]...) while((s32[]{:T(128)}, f32[1,8,64,128]{3,2,1,0:T(8,128)S(1)}, ...), condition=%wide.region_4.5_spmd.clone.clone, body=%wide.region_1.4_spmd.clone.clone.sunk | while | flops 909582336 | bytes 5468616 | solution.py:57
  108.3 4.4 fusion.288
  119.3 4.5 fusion.288
  130.4 4.4 fusion.288
  141.4 4.4 fusion.288
  145.8 3.8 copy.169
  149.7 4.8 reshape.1130
  154.5 6.6 %multiply_reduce_fusion.9 = (f32[1024]{0:T(1024)S(1)}, f32[1024,512]{1,0:T(8,128)}, f32[1024,512]{1,0:T(8,128)}) fusion(f32[1024,512]{1,0:T(8,128)} %reshape.1130, f32[1,1024,512]{2,1,0:T(8,128)S(1)} %get-tuple-element.802, f32[512]{0:T(512)S(1)} %mul.811, bf16[1024,1024]{1,0:T(8,128)(2,1)} %all-gather.6.cloned.1.call-done, ...), kind=kOutput, calls=%fused_computation.199 | convolution fusion | flops 1080556544 | bytes 11540480 | tf_op jit(solution)/shard_map/dot_general | solution.py:85
  161.1 9.0 %psum.56 = f32[1024]{0:T(1024)S(1)} all-reduce(f32[1024]{0:T(1024)S(1)} %get-tuple-element.797), channel_id=1, replica_groups=mesh['dp'=8,'tensor'=4] {'tensor'}, use_global_device_ids=true, to_apply=%region_6.7 | all-reduce | flops 1024 | bytes 8192 | tf_op jit(solution)/shard_map/psum | solution.py:153
  170.1 9.8 %all-gather.14.cloned.1.call-done = bf16[1024,1024]{1,0:T(8,128)(2,1)} async-done(((bf16[256,1024]{1,0:T(8,128)(2,1)}), bf16[1024,1024]{1,0:T(8,128)(2,1)}) %all-gather.14.cloned.1.call-update) | async-done | bytes 2097168 | tf_op jit(solution)/shard_map/all_gather | solution.py:161
  179.9 5.9 multiply_reduce_fusion.3
  185.8 10.4 %psum.57 = f32[1024]{0:T(1024)S(1)} all-reduce(f32[1024]{0:T(1024)S(1)} %get-tuple-element.715), channel_id=1, replica_groups=mesh['dp'=8,'tensor'=4] {'tensor'}, use_global_device_ids=true, to_apply=%region_9.10 | all-reduce | flops 1024 | bytes 8192 | tf_op jit(solution)/shard_map/psum | solution.py:166
  196.2 5.4 fusion.134
  201.6 4.4 reshape.1131
  206.0 3.8 copy.160
  213.6 107.7 %while.43 = (s32[]{:T(128)}, f32[8]{0:T(128)}, f32[1,8,64,128]{3,2,1,0:T(8,128)S(1)}, f32[4,1,256,8,64]{2,4,3,1,0:T(8,128)}, f32[4,1,256,8]{2,3,1,0:T(8,128)}, /...) while((s32[]{:T(128)}, f32[8]{0:T(128)}, ...), condition=%wide.region_23.24_spmd.clone, body=%wide.region_10.23_spmd.clone.sunk | while | flops 2126555136 | bytes 16984652 | solution.py:57
  221.7 4.1 fusion.266
  230.9 2.5 reduce-window.74
  236.3 3.8 fusion.272
  248.1 4.1 fusion.266
  257.3 2.5 reduce-window.74
  263.3 3.8 fusion.272
  275.1 4.1 fusion.266
  290.4 3.8 fusion.272
  302.2 4.1 fusion.266
  317.4 3.8 fusion.272
  328.8 31.8 %reduce-scatter.20.cloned.1.call-done = bf16[128,256]{1,0:T(8,128)(2,1)} async-done(((bf16[1024,256]{1,0:T(8,128)(2,1)}), bf16[128,256]{1,0:T(8,128)(2,1)}) %reduce-scatter.20.cloned.1.call-update) | async-done | bytes 65552 | tf_op jit(solution)/shard_map/reduce_scatter | solution.py:197
  360.7 4.6 convolution_convert_fusion.1
  367.8 2.8 copy.172
  370.6 5.0 reshape.1132
  375.6 4.6 fusion.130
  383.5 3.8 multiply_reduce_fusion.7
  400.8 3.8 convolution_convert_fusion
  408.3 26.2 %all-reduce.30.cloned.1.call-done = bf16[128,256]{1,0:T(8,128)(2,1)} async-done(((bf16[128,256]{1,0:T(8,128)(2,1)}), bf16[128,256]{1,0:T(8,128)(2,1)}) %all-reduce.30.cloned.1.call-update) | async-done | bytes 65552 | tf_op jit(solution)/shard_map/psum | solution.py:207
  435.9 37.8 %reduce-scatter.24.cloned.1.call-done = bf16[128,512]{1,0:T(8,128)(2,1)} async-done(((bf16[1024,512]{1,0:T(8,128)(2,1)}), bf16[128,512]{1,0:T(8,128)(2,1)}) %reduce-scatter.24.cloned.1.call-update) | async-done | bytes 131088
  475.5 38.2 %reduce-scatter.16.cloned.1.call-done = bf16[128,512]{1,0:T(8,128)(2,1)} async-done(((bf16[1024,512]{1,0:T(8,128)(2,1)}), bf16[128,512]{1,0:T(8,128)(2,1)}) %reduce-scatter.16.cloned.1.call-update) | async-done | bytes 131088 | tf_op jit(solution)/shard_map/reduce_scatter | solution.py:191
  515.3 37.9 %reduce-scatter.18.cloned.1.call-done = bf16[128,512]{1,0:T(8,128)(2,1)} async-done(((bf16[1024,512]{1,0:T(8,128)(2,1)}), bf16[128,512]{1,0:T(8,128)(2,1)}) %reduce-scatter.18.cloned.1.call-update) | async-done | bytes 131088 | tf_op jit(solution)/shard_map/reduce_scatter | solution.py:194
  554.9 42.3 %reduce-scatter.14.cloned.1.call-done = bf16[256,1024]{1,0:T(8,128)(2,1)} async-done(((bf16[1024,1024]{1,0:T(8,128)(2,1)}), bf16[256,1024]{1,0:T(8,128)(2,1)}) %reduce-scatter.14.cloned.1.call-update) | async-done | bytes 524304 | tf_op jit(solution)/shard_map/reduce_scatter | solution.py:177
  598.6 47.7 %all-reduce.27 = (f32[1024]{0:T(1024)}, f32[5,2048]{1,0:T(8,128)S(1)}, f32[5,256]{1,0:T(8,128)}, f32[3,32]{1,0:T(4,128)S(1)}, f32[2048]{0:T(1024)S(1)}) all-reduce(f32[1024]{0:T(1024)S(1)} %get-tuple-element.732, f32[5,2048]{1,0:T(8,128)S(1)} %add_dynamic-update-slice_fusion, ...), channel_id=1, replica_groups=mesh['dp'=8,'tensor'=4] {'dp','tensor'}, use_global_device_ids=true, to_apply=%region_27.28 | all-reduce | flops 14688 | bytes 117504 | tf_op jit(solution)/shard_map/psum | solution.py:210
  648.2 3.0 fusion.140
  (444 shorter events, 158.3 us)
Async XLA Ops:
  7.2 7.3 %copy-start.61 = (f32[3,8]{1,0:T(4,128)S(1)}, f32[3,8]{1,0:T(4,128)}, u32[]{:S(2)}) copy-start(f32[3,8]{1,0:T(4,128)} %param.25) | copy-start | bytes 292
  7.2 8.7 %copy-start.58 = (f32[5,256]{1,0:T(8,128)S(1)}, f32[5,256]{1,0:T(8,128)}, u32[]{:S(2)}) copy-start(f32[5,256]{1,0:T(8,128)} %param.24) | copy-start | bytes 15364
  7.2 8.7 %copy-start.56 = (f32[5,512]{1,0:T(8,128)S(1)}, f32[5,512]{1,0:T(8,128)}, u32[]{:S(2)}) copy-start(f32[5,512]{1,0:T(8,128)} %param.23) | copy-start | bytes 30724
  7.2 8.8 %copy-start.59 = (bf16[128,8]{0,1:T(8,128)(2,1)S(1)}, bf16[128,8]{0,1:T(8,128)(2,1)}, u32[]{:S(2)}) copy-start(bf16[128,8]{0,1:T(8,128)(2,1)} %param.22) | copy-start | bytes 6148
  7.2 17.7 %copy-start.23 = (bf16[128,256]{1,0:T(8,128)(2,1)S(1)}, bf16[128,256]{1,0:T(8,128)(2,1)}, u32[]{:S(2)}) copy-start(bf16[128,256]{1,0:T(8,128)(2,1)} %param.21) | copy-start | bytes 196612
  7.2 50.1 %all-gather.6.cloned.1.call-start = ((), (), s32[]{:S(2)}) async-start(), calls=%async_computation.7 | async-start | bytes 2621440 | tf_op jit(solution)/shard_map/all_gather | solution.py:130
  11.7 71.4 %all-gather.8.cloned.1.call-start = ((), (), s32[]{:S(2)}) async-start(), calls=%async_computation.8 | async-start | bytes 1179648 | tf_op jit(solution)/shard_map/all_gather | solution.py:135
  12.5 142.0 %all-gather.10.cloned.1.call-start = ((), (), s32[]{:S(2)}) async-start(), calls=%async_computation.9 | async-start | bytes 1179648 | tf_op jit(solution)/shard_map/all_gather | solution.py:134
  13.2 156.9 %all-gather.12.cloned.1.call-start = ((), (), s32[]{:S(2)}) async-start(), calls=%async_computation.10 | async-start | bytes 1179648 | tf_op jit(solution)/shard_map/all_gather | solution.py:138
  13.8 166.1 %all-gather.14.cloned.1.call-start = ((), (), s32[]{:S(2)}) async-start(), calls=%async_computation.12 | async-start | bytes 2621440 | tf_op jit(solution)/shard_map/all_gather | solution.py:161
  14.4 346.3 %reduce-scatter.20.cloned.1.call-start = ((), (), s32[]{:S(2)}) async-start(), calls=%async_computation.16 | async-start | bytes 589824 | tf_op jit(solution)/shard_map/reduce_scatter | solution.py:197
  15.9 138.6 %copy-start.32 = (f32[512]{0:T(512)}, f32[512]{0:T(512)S(1)}, u32[]{:S(2)}) copy-start(f32[512]{0:T(512)S(1)} %mul.811) | copy-start | bytes 6148
  15.9 43.8 %copy-start.45 = (f32[1,256]{1,0:T(1,128)}, f32[1,256]{1,0:T(1,128)S(1)}, u32[]{:S(2)}) copy-start(f32[1,256]{1,0:T(1,128)S(1)} %get-tuple-element.831) | copy-start | bytes 3076
  15.9 43.8 %copy-start.47 = (f32[1,256]{1,0:T(1,128)}, f32[1,256]{1,0:T(1,128)S(1)}, u32[]{:S(2)}) copy-start(f32[1,256]{1,0:T(1,128)S(1)} %get-tuple-element.832) | copy-start | bytes 3076
  15.9 43.8 %copy-start.49 = (f32[1,256]{1,0:T(1,128)}, f32[1,256]{1,0:T(1,128)S(1)}, u32[]{:S(2)}) copy-start(f32[1,256]{1,0:T(1,128)S(1)} %get-tuple-element.833) | copy-start | bytes 3076
  15.9 43.8 %copy-start.51 = (f32[1,256]{1,0:T(1,128)}, f32[1,256]{1,0:T(1,128)S(1)}, u32[]{:S(2)}) copy-start(f32[1,256]{1,0:T(1,128)S(1)} %get-tuple-element.834) | copy-start | bytes 3076
  16.0 69.6 %copy-start.34 = (f32[1,512]{1,0:T(1,128)}, f32[1,512]{1,0:T(1,128)S(1)}, u32[]{:S(2)}) copy-start(f32[1,512]{1,0:T(1,128)S(1)} %get-tuple-element.826) | copy-start | bytes 6148
  16.0 69.6 %copy-start.36 = (f32[1,512]{1,0:T(1,128)}, f32[1,512]{1,0:T(1,128)S(1)}, u32[]{:S(2)}) copy-start(f32[1,512]{1,0:T(1,128)S(1)} %get-tuple-element.827) | copy-start | bytes 6148
  16.0 69.6 %copy-start.38 = (f32[1,512]{1,0:T(1,128)}, f32[1,512]{1,0:T(1,128)S(1)}, u32[]{:S(2)}) copy-start(f32[1,512]{1,0:T(1,128)S(1)} %get-tuple-element.828) | copy-start | bytes 6148
  16.0 69.6 %copy-start.40 = (f32[1,512]{1,0:T(1,128)}, f32[1,512]{1,0:T(1,128)S(1)}, u32[]{:S(2)}) copy-start(f32[1,512]{1,0:T(1,128)S(1)} %get-tuple-element.829) | copy-start | bytes 6148
  24.9 72.3 %copy-start.19 = (bf16[1024,8]{0,1:T(8,128)(2,1)}, bf16[1024,8]{0,1:T(8,128)(2,1)S(1)}, u32[]{:S(2)}) copy-start(bf16[1024,8]{0,1:T(8,128)(2,1)S(1)} %all_gather.22) | copy-start | bytes 49156
  33.8 25.9 %copy-start.14 = (bf16[1024,256]{1,0:T(8,128)(2,1)}, bf16[1024,256]{1,0:T(8,128)(2,1)S(1)}, u32[]{:S(2)}) copy-start(bf16[1024,256]{1,0:T(8,128)(2,1)S(1)} %all_gather.24) | copy-start | bytes 1572868
  61.4 21.8 %copy-start.6 = (bf16[1024,1024]{1,0:T(8,128)(2,1)S(1)}, bf16[1024,1024]{1,0:T(8,128)(2,1)}, u32[]{:S(2)}) copy-start(bf16[1024,1024]{1,0:T(8,128)(2,1)} %all-gather.6.cloned.1.call-done) | copy-start | bytes 6291460
  88.3 107.9 %copy-start.2 = (f32[1,1024,512]{2,1,0:T(8,128)}, f32[1,1024,512]{2,1,0:T(8,128)S(1)}, u32[]{:S(2)}) copy-start(f32[1,1024,512]{2,1,0:T(8,128)S(1)} %get-tuple-element.802) | copy-start | bytes 6291460
  102.5 5.8 copy-start.24
  113.6 5.8 copy-start.24
  124.6 5.8 copy-start.24
  154.5 25.4 %copy-start.54 = (f32[512]{0:T(512)S(1)}, f32[512]{0:T(512)}, u32[]{:S(2)}) copy-start(f32[512]{0:T(512)} %param.26) | copy-start | bytes 6148
  170.1 26.1 %copy-start.25 = (f32[1024]{0:T(1024)}, f32[1024]{0:T(1024)S(1)}, u32[]{:S(2)}) copy-start(f32[1024]{0:T(1024)S(1)} %get-tuple-element.836) | copy-start | bytes 12292
  170.1 26.2 %copy-start.27 = (f32[1024]{0:T(1024)}, f32[1024]{0:T(1024)S(1)}, u32[]{:S(2)}) copy-start(f32[1024]{0:T(1024)S(1)} %get-tuple-element.835) | copy-start | bytes 12292
  218.8 7.0 %copy-start.18 = (f32[8,256]{1,0:T(8,128)}, f32[8,256]{1,0:T(8,128)S(1)}, u32[]{:S(2)}) copy-start(f32[8,256]{1,0:T(8,128)S(1)} %bitcast_add_fusion.13) | copy-start | bytes 24580 | tf_op jit(solution)/shard_map/transpose(jvp(vmap()))/while
  245.2 7.0 %copy-start.18 = (f32[8,256]{1,0:T(8,128)}, f32[8,256]{1,0:T(8,128)S(1)}, u32[]{:S(2)}) copy-start(f32[8,256]{1,0:T(8,128)S(1)} %bitcast_add_fusion.13) | copy-start | bytes 24580 | tf_op jit(solution)/shard_map/transpose(jvp(vmap()))/while
  272.3 7.0 %copy-start.18 = (f32[8,256]{1,0:T(8,128)}, f32[8,256]{1,0:T(8,128)S(1)}, u32[]{:S(2)}) copy-start(f32[8,256]{1,0:T(8,128)S(1)} %bitcast_add_fusion.13) | copy-start | bytes 24580 | tf_op jit(solution)/shard_map/transpose(jvp(vmap()))/while
  299.3 7.0 %copy-start.18 = (f32[8,256]{1,0:T(8,128)}, f32[8,256]{1,0:T(8,128)S(1)}, u32[]{:S(2)}) copy-start(f32[8,256]{1,0:T(8,128)S(1)} %bitcast_add_fusion.13) | copy-start | bytes 24580 | tf_op jit(solution)/shard_map/transpose(jvp(vmap()))/while
  327.3 33.4 %copy-start.26 = (f32[1024]{0:T(1024)S(1)}, f32[1024]{0:T(1024)}, u32[]{:S(2)}) copy-start(f32[1024]{0:T(1024)} %copy-done.25) | copy-start | bytes 12292
  327.3 33.5 %copy-start.55 = (f32[512]{0:T(512)S(1)}, f32[512]{0:T(512)}, u32[]{:S(2)}) copy-start(f32[512]{0:T(512)} %param.26) | copy-start | bytes 6148
  327.3 79.5 %reduce-scatter.22.cloned.1.call-start = ((), (), s32[]{:S(2)}) async-start(), calls=%async_computation.18 | async-start | bytes 294912
  328.8 105.7 %all-reduce.30.cloned.1.call-start = ((), (), s32[]{:S(2)}) async-start(), calls=%async_computation.17 | async-start | bytes 131072 | tf_op jit(solution)/shard_map/psum | solution.py:207
  360.7 113.1 %reduce-scatter.24.cloned.1.call-start = ((), (), s32[]{:S(2)}) async-start(), calls=%async_computation.19 | async-start | bytes 1179648
  367.8 145.9 %reduce-scatter.16.cloned.1.call-start = ((), (), s32[]{:S(2)}) async-start(), calls=%async_computation.14 | async-start | bytes 1179648 | tf_op jit(solution)/shard_map/reduce_scatter | solution.py:191
  383.5 169.8 %reduce-scatter.18.cloned.1.call-start = ((), (), s32[]{:S(2)}) async-start(), calls=%async_computation.15 | async-start | bytes 1179648 | tf_op jit(solution)/shard_map/reduce_scatter | solution.py:194
  392.6 204.6 %reduce-scatter.14.cloned.1.call-start = ((), (), s32[]{:S(2)}) async-start(), calls=%async_computation.13 | async-start | bytes 2621440 | tf_op jit(solution)/shard_map/reduce_scatter | solution.py:177
  399.2 249.0 %reduce-scatter.12.cloned.1.call-start = ((), (), s32[]{:S(2)}) async-start(), calls=%async_computation.11 | async-start | bytes 2621440 | tf_op jit(solution)/shard_map/reduce_scatter | solution.py:158
  404.6 192.6 %copy-start.5 = (bf16[256,1024]{1,0:T(8,128)(2,1)S(1)}, bf16[256,1024]{1,0:T(8,128)(2,1)}, u32[]{:S(2)}) copy-start(bf16[256,1024]{1,0:T(8,128)(2,1)} %param.16) | copy-start | bytes 1572868
  404.6 192.6 %copy-start.31 = (f32[1024]{0:T(1024)S(1)}, f32[1024]{0:T(1024)}, u32[]{:S(2)}) copy-start(f32[1024]{0:T(1024)} %param.18) | copy-start | bytes 12292
  404.6 192.6 %copy-start.43 = (f32[256]{0:T(256)S(1)}, f32[256]{0:T(256)}, u32[]{:S(2)}) copy-start(f32[256]{0:T(256)} %copy-done.42) | copy-start | bytes 3076
  404.6 243.6 %copy-start.13 = (bf16[256,1024]{1,0:T(8,128)(2,1)S(1)}, bf16[256,1024]{1,0:T(8,128)(2,1)}, u32[]{:S(2)}) copy-start(bf16[256,1024]{1,0:T(8,128)(2,1)} %param.17) | copy-start | bytes 1572868
  404.7 243.6 %copy-start.57 = (f32[256]{0:T(256)S(1)}, f32[256]{0:T(256)}, u32[]{:S(2)}) copy-start(f32[256]{0:T(256)} %get-tuple-element.840) | copy-start | bytes 3076
  (38 other events, 110.4 us)
Sparse Core Ops, SparseCore 0:
  11.9 45.4 all-gather.5
  59.3 23.7 all-gather.7
  85.0 23.4 all-gather.9
  110.3 23.5 all-gather.11
  135.3 44.5 all-gather.13
  327.4 33.1 reduce-scatter.19
  364.5 33.5 reduce-scatter.21
  400.5 33.9 all-reduce.29
  437.9 35.7 reduce-scatter.23
  477.7 35.9 reduce-scatter.15
  517.2 36.0 reduce-scatter.17
  555.5 41.5 reduce-scatter.13
  599.5 44.2 reduce-scatter.11
where the time goes:
time: 665 us; the launch traced here: 658 us
  waiting for transfers between devices  271 us (41%)
  matrix products  129 us (19%)
  blocking collectives  84.9 us (13%)
  other arithmetic  80.9 us (12%)
  local copies, waits for them, and re-layouts  76.1 us (11%)
  between operations  15.1 us (2%)
    dot_general x12, matrix products, span_step(): within = jnp.einsum('hij,jhp->ihp', kernel, block_values, precision=HIGHEST)  49.3 us
    psum x1, blocking collectives, body(): lax.psum((place(mix_grads[4], INNER), place(mix_grads[6], HEADS), grad_gn...  47.7 us
    reduce_scatter x1, waiting for transfers between devices, body(): lax.psum_scatter(grad_normed.astype(jnp.bfloat16), 'tensor', scatter_dime...  42.3 us
    unnamed x15, waiting for transfers between devices  40.4 us
    reduce_scatter x1, waiting for transfers between devices, body(): lax.psum_scatter(weight_terms[0].astype(jnp.bfloat16), 'dp', scatter_dime...  38.2 us
    reduce_scatter x1, waiting for transfers between devices, body(): lax.psum_scatter(weight_terms[1].astype(jnp.bfloat16), 'dp', scatter_dime...  37.9 us
    reduce_scatter x1, waiting for transfers between devices, body(): lax.psum_scatter(weight_terms[2].astype(jnp.bfloat16), 'dp', scatter_dime...  31.8 us
    psum x1, waiting for transfers between devices, body(): lax.psum(summed[2].astype(jnp.bfloat16), 'tensor').astype(jnp.float32)  26.2 us
  transfers between devices with their start and end apart: 13, of which 9 were waited for; matrix products, arithmetic and copies ran while one was open for 21% of the time, Pallas kernels for 0%

commit v1 on v0

--- a/solution.py
+++ b/solution.py
@@ -10,6 +10,19 @@
 INNER = 2048
 EPSILON = 1e-05
 HIGHEST = lax.Precision.HIGHEST
+
+
+def gather_around(x, axis, dim):
+    ways = lax.axis_size(axis)
+    up = [(d, (d + 1) % ways) for d in range(ways)]
+    down = [(d, (d - 1) % ways) for d in range(ways)]
+    earlier, later = ([x], [x])
+    for _ in range(ways // 2):
+        earlier.append(lax.ppermute(earlier[-1], axis, up))
+    for _ in range((ways - 1) // 2):
+        later.append(lax.ppermute(later[-1], axis, down))
+    line = jnp.concatenate([*earlier[::-1], *later[1:]], axis=dim)
+    return jnp.roll(line, (lax.axis_index(axis) - ways // 2) * x.shape[dim], axis=dim)
 
 
 def causal(sequence, taps):
@@ -127,9 +140,7 @@
     rows32 = tokens.astype(jnp.float32)
     grad_out = cotangent.astype(jnp.float32)
     scaling = lax.rsqrt(jnp.mean(rows32 * rows32, axis=1, keepdims=True) + EPSILON)
-    normed = lax.all_gather(
-        (rows32 * scaling * norm_gain).astype(jnp.bfloat16), "tensor", axis=0, tiled=True
-    )
+    normed = gather_around((rows32 * scaling * norm_gain).astype(jnp.bfloat16), "tensor", 0)
     fetched = (
         lax.all_gather(w_gate, "dp", axis=0, tiled=True),
         lax.all_gather(w_value, "dp", axis=0, tiled=True),

time: 665 us -> 625 us (0.940)
  waiting for transfers between devices: 271 us -> 231 us
  other arithmetic: 80.9 us -> 70.5 us
    all_gather x1 -> x0, waiting for transfers between devices: 23.6 us -> none  [body(): lax.all_gather((rows32 * scaling * norm_gain).astype(jnp.bfloat16), 'tens...]
    all_gather x1, waiting for transfers between devices: 20.7 us -> 0.01 us  [body(): lax.all_gather(w_value, 'dp', axis=0, tiled=True)]
    ppermute x0 -> x3, waiting for transfers between devices: none -> 16.2 us  [the longest x2 16.2 us: gather_around(): earlier.append(lax.ppermute(earlier[-1], axis, up))]
    all_gather x1, waiting for transfers between devices: 9.82 us -> 0.02 us  [body(): grad_rows = lax.all_gather(cotangent, 'tensor', axis=0, tiled=True)]
    another operation x52, other arithmetic: 25.5 us -> 17.5 us
    unnamed x128 -> x143, local copies, waits for them, and re-layouts: 19.1 us -> 20 us
    unnamed x15 -> x14, waiting for transfers between devices: 40.4 us -> 40 us
  transfers between devices with their start and end apart: 13 -> 15, of which waited for: 9 -> 8; matrix products, arithmetic and copies ran while one was open for 21% -> 23% of each run, Pallas kernels for 0% -> 0%
where the time goes in v1:
time: 625 us; the launch traced here: 617 us
  waiting for transfers between devices  231 us (37%)
  matrix products  134 us (21%)
  blocking collectives  85.3 us (14%)
  local copies, waits for them, and re-layouts  76.4 us (12%)
  other arithmetic  70.5 us (11%)
  between operations  15.6 us (2%)
    dot_general x12, matrix products, span_step(): within = jnp.einsum('hij,jhp->ihp', kernel, block_values, precision=HIGHEST)  49.8 us
    psum x1, blocking collectives, body(): lax.psum((place(mix_grads[4], INNER), place(mix_grads[6], HEADS), grad_gn...  47.6 us
    reduce_scatter x1, waiting for transfers between devices, body(): lax.psum_scatter(grad_normed.astype(jnp.bfloat16), 'tensor', scatter_dime...  42.4 us
    unnamed x14, waiting for transfers between devices  40 us
    reduce_scatter x1, waiting for transfers between devices, body(): lax.psum_scatter(weight_terms[0].astype(jnp.bfloat16), 'dp', scatter_dime...  38.4 us
    reduce_scatter x1, waiting for transfers between devices, body(): lax.psum_scatter(weight_terms[1].astype(jnp.bfloat16), 'dp', scatter_dime...  37.7 us
    reduce_scatter x1, waiting for transfers between devices, body(): lax.psum_scatter(weight_terms[2].astype(jnp.bfloat16), 'dp', scatter_dime...  30.4 us
    psum x1, waiting for transfers between devices, body(): lax.psum(summed[2].astype(jnp.bfloat16), 'tensor').astype(jnp.float32)  26.1 us
  transfers between devices with their start and end apart: 15, of which 8 were waited for; matrix products, arithmetic and copies ran while one was open for 23% of the time, Pallas kernels for 0%

profile of v1, /device:TPU:10, one launch (start us, length us, event | category | flops | bytes accessed | tf_op | source)
XLA Modules:
  0.0 616.5 jit_solution(13037789324560379097)
XLA Ops:
  14.8 9.9 %all_gather.20 = bf16[1024,256]{1,0:T(8,128)(2,1)S(1)} all-gather(bf16[128,256]{1,0:T(8,128)(2,1)S(1)} %copy-done.29), channel_id=1, replica_groups=mesh['dp'=8,'tensor'=4] {'dp'}, dimensions={0}, use_global_device_ids=true | all-gather | bytes 589824 | tf_op jit(solution)/shard_map/all_gather | solution.py:147
  25.3 14.4 %collective-permute-done = bf16[256,1024]{1,0:T(8,128)(2,1)S(1)} collective-permute-done((bf16[256,1024]{1,0:T(8,128)(2,1)S(1)}, bf16[256,1024]{1,0:T(8,128)(2,1)S(1)}, u32[]{:S(2)}, u32[]{:S(2)}) %collective-permute-start) | collective-permute-done | bytes 524320 | tf_op jit(solution)/shard_map/ppermute | solution.py:21
  41.8 8.9 %all_gather.18 = bf16[1024,8]{0,1:T(8,128)(2,1)S(1)} all-gather(bf16[128,8]{0,1:T(8,128)(2,1)S(1)} %copy-done.68), channel_id=1, replica_groups=mesh['dp'=8,'tensor'=4] {'dp'}, dimensions={0}, use_global_device_ids=true | all-gather | bytes 18432 | tf_op jit(solution)/shard_map/all_gather | solution.py:148
  58.2 3.1 fusion.165
  61.4 2.6 fusion.137
  64.1 5.1 reshape.1137
  69.2 3.9 copy.149
  74.6 44.1 %while.44 = (s32[]{:T(128)}, f32[1,8,64,128]{3,2,1,0:T(8,128)S(1)}, f32[4,1,256,8,64]{2,4,3,1,0:T(8,128)}, f32[4,1,8,64,128]{4,3,2,1,0:T(8,128)}, f32[4,1,256,8]...) while((s32[]{:T(128)}, f32[1,8,64,128]{3,2,1,0:T(8,128)S(1)}, ...), condition=%wide.region_4.5_spmd.clone.clone, body=%wide.region_1.4_spmd.clone.clone.sunk | while | flops 909582336 | bytes 5206444 | solution.py:70
  81.3 4.4 fusion.297
  92.3 4.4 fusion.297
  103.3 4.4 fusion.297
  114.3 4.4 fusion.297
  118.8 3.9 copy.169
  122.6 4.8 reshape.1130
  127.5 6.5 %multiply_reduce_fusion.9 = (f32[1024]{0:T(1024)S(1)}, f32[1024,512]{1,0:T(8,128)}, f32[1024,512]{1,0:T(8,128)}) fusion(f32[1024,512]{1,0:T(8,128)} %reshape.1130, f32[1,1024,512]{2,1,0:T(8,128)S(1)} %get-tuple-element.802, f32[512]{0:T(512)S(1)} %copy-done.48, bf16[1024,512]{1,0:T(8,128)(2,1)} %all-gather.7.cloned.1.call-done, ...), kind=kOutput, calls=%fused_computation.199 | convolution fusion | flops 1080556544 | bytes 11540484 | tf_op jit(solution)/shard_map/dot_general | solution.py:98
  134.0 10.3 %psum.56 = f32[1024]{0:T(1024)S(1)} all-reduce(f32[1024]{0:T(1024)S(1)} %get-tuple-element.797), channel_id=1, replica_groups=mesh['dp'=8,'tensor'=4] {'tensor'}, use_global_device_ids=true, to_apply=%region_6.7 | all-reduce | flops 1024 | bytes 8192 | tf_op jit(solution)/shard_map/psum | solution.py:164
  144.4 5.9 multiply_reduce_fusion.3
  150.3 8.6 %psum.57 = f32[1024]{0:T(1024)S(1)} all-reduce(f32[1024]{0:T(1024)S(1)} %get-tuple-element.715), channel_id=1, replica_groups=mesh['dp'=8,'tensor'=4] {'tensor'}, use_global_device_ids=true, to_apply=%region_9.10 | all-reduce | flops 1024 | bytes 8192 | tf_op jit(solution)/shard_map/psum | solution.py:177
  159.0 5.3 fusion.134
  164.2 4.4 reshape.1131
  168.6 3.8 copy.160
  176.3 102.2 %while.43 = (s32[]{:T(128)}, f32[8]{0:T(128)}, f32[1,8,64,128]{3,2,1,0:T(8,128)}, f32[4,1,256,8,64]{2,4,3,1,0:T(8,128)}, f32[4,1,256,8]{2,3,1,0:T(8,128)}, /*ind...) while((s32[]{:T(128)}, f32[8]{0:T(128)}, ...), condition=%wide.region_23.24_spmd.clone, body=%wide.region_10.23_spmd.clone.sunk | while | flops 2126555136 | bytes 17050868 | solution.py:70
  184.5 4.1 fusion.275
  192.5 2.5 reduce-window.74
  197.2 3.9 fusion.281
  210.2 4.1 fusion.275
  218.2 2.5 reduce-window.74
  223.0 3.9 fusion.281
  235.9 4.1 fusion.275
  243.9 2.5 reduce-window.74
  248.7 3.9 fusion.281
  261.7 4.1 fusion.275
  269.7 2.5 reduce-window.74
  274.4 3.9 fusion.281
  288.4 30.4 %reduce-scatter.20.cloned.1.call-done = bf16[128,256]{1,0:T(8,128)(2,1)} async-done(((bf16[1024,256]{1,0:T(8,128)(2,1)}), bf16[128,256]{1,0:T(8,128)(2,1)}) %reduce-scatter.20.cloned.1.call-update) | async-done | bytes 65552 | tf_op jit(solution)/shard_map/reduce_scatter | solution.py:208
  318.9 3.9 convolution_convert_fusion.1
  325.4 2.8 copy.172
  328.2 5.0 reshape.1132
  333.2 4.6 fusion.130
  341.1 3.8 multiply_reduce_fusion.7
  359.0 3.8 convolution_convert_fusion
  366.4 26.1 %all-reduce.30.cloned.1.call-done = bf16[128,256]{1,0:T(8,128)(2,1)} async-done(((bf16[128,256]{1,0:T(8,128)(2,1)}), bf16[128,256]{1,0:T(8,128)(2,1)}) %all-reduce.30.cloned.1.call-update) | async-done | bytes 65552 | tf_op jit(solution)/shard_map/psum | solution.py:218
  394.0 37.8 %reduce-scatter.24.cloned.1.call-done = bf16[128,512]{1,0:T(8,128)(2,1)} async-done(((bf16[1024,512]{1,0:T(8,128)(2,1)}), bf16[128,512]{1,0:T(8,128)(2,1)}) %reduce-scatter.24.cloned.1.call-update) | async-done | bytes 131088
  433.5 38.4 %reduce-scatter.16.cloned.1.call-done = bf16[128,512]{1,0:T(8,128)(2,1)} async-done(((bf16[1024,512]{1,0:T(8,128)(2,1)}), bf16[128,512]{1,0:T(8,128)(2,1)}) %reduce-scatter.16.cloned.1.call-update) | async-done | bytes 131088 | tf_op jit(solution)/shard_map/reduce_scatter | solution.py:202
  473.5 37.7 %reduce-scatter.18.cloned.1.call-done = bf16[128,512]{1,0:T(8,128)(2,1)} async-done(((bf16[1024,512]{1,0:T(8,128)(2,1)}), bf16[128,512]{1,0:T(8,128)(2,1)}) %reduce-scatter.18.cloned.1.call-update) | async-done | bytes 131088 | tf_op jit(solution)/shard_map/reduce_scatter | solution.py:205
  512.9 42.4 %reduce-scatter.14.cloned.1.call-done = bf16[256,1024]{1,0:T(8,128)(2,1)} async-done(((bf16[1024,1024]{1,0:T(8,128)(2,1)}), bf16[256,1024]{1,0:T(8,128)(2,1)}) %reduce-scatter.14.cloned.1.call-update) | async-done | bytes 524304 | tf_op jit(solution)/shard_map/reduce_scatter | solution.py:188
  556.7 47.6 %all-reduce.27 = (f32[1024]{0:T(1024)}, f32[5,2048]{1,0:T(8,128)S(1)}, f32[5,256]{1,0:T(8,128)}, f32[3,32]{1,0:T(4,128)S(1)}, f32[2048]{0:T(1024)S(1)}) all-reduce(f32[1024]{0:T(1024)S(1)} %get-tuple-element.732, f32[5,2048]{1,0:T(8,128)S(1)} %add_dynamic-update-slice_fusion, ...), channel_id=1, replica_groups=mesh['dp'=8,'tensor'=4] {'dp','tensor'}, use_global_device_ids=true, to_apply=%region_27.28 | all-reduce | flops 14688 | bytes 117504 | tf_op jit(solution)/shard_map/psum | solution.py:221
  606.3 3.0 fusion.140
  (505 shorter events, 151.5 us)
Async XLA Ops:
  7.2 7.6 %copy-start.29 = (bf16[128,256]{1,0:T(8,128)(2,1)S(1)}, bf16[128,256]{1,0:T(8,128)(2,1)}, u32[]{:S(2)}) copy-start(bf16[128,256]{1,0:T(8,128)(2,1)} %param.21) | copy-start | bytes 196612
  7.2 17.5 %copy-start.71 = (f32[3,8]{1,0:T(4,128)S(1)}, f32[3,8]{1,0:T(4,128)}, u32[]{:S(2)}) copy-start(f32[3,8]{1,0:T(4,128)} %param.25) | copy-start | bytes 292
  7.2 18.0 %copy-start.67 = (f32[5,256]{1,0:T(8,128)S(1)}, f32[5,256]{1,0:T(8,128)}, u32[]{:S(2)}) copy-start(f32[5,256]{1,0:T(8,128)} %param.24) | copy-start | bytes 15364
  7.2 32.5 %copy-start.65 = (f32[5,512]{1,0:T(8,128)S(1)}, f32[5,512]{1,0:T(8,128)}, u32[]{:S(2)}) copy-start(f32[5,512]{1,0:T(8,128)} %param.23) | copy-start | bytes 30724
  7.2 34.5 %copy-start.68 = (bf16[128,8]{0,1:T(8,128)(2,1)S(1)}, bf16[128,8]{0,1:T(8,128)(2,1)}, u32[]{:S(2)}) copy-start(bf16[128,8]{0,1:T(8,128)(2,1)} %param.22) | copy-start | bytes 6148
  7.2 51.0 %all-gather.5.cloned.1.call-start = ((), (), s32[]{:S(2)}) async-start(), calls=%async_computation.7 | async-start | bytes 1179648 | tf_op jit(solution)/shard_map/all_gather | solution.py:146
  8.0 119.5 %all-gather.7.cloned.1.call-start = ((), (), s32[]{:S(2)}) async-start(), calls=%async_computation.8 | async-start | bytes 1179648 | tf_op jit(solution)/shard_map/all_gather | solution.py:145
  8.7 135.6 %all-gather.9.cloned.1.call-start = ((), (), s32[]{:S(2)}) async-start(), calls=%async_computation.9 | async-start | bytes 1179648 | tf_op jit(solution)/shard_map/all_gather | solution.py:149
  9.4 134.9 %all-gather.11.cloned.1.call-start = ((), (), s32[]{:S(2)}) async-start(), calls=%async_computation.11 | async-start | bytes 2621440 | tf_op jit(solution)/shard_map/all_gather | solution.py:172
  11.3 41.6 %copy-start.38 = (f32[256]{0:T(256)}, f32[256]{0:T(256)S(1)}, u32[]{:S(2)}) copy-start(f32[256]{0:T(256)S(1)} %get-tuple-element.841) | copy-start | bytes 3076
  11.3 41.3 %copy-start.4 = (bf16[256,1024]{1,0:T(8,128)(2,1)S(1)}, bf16[256,1024]{1,0:T(8,128)(2,1)}, u32[]{:S(2)}) copy-start(bf16[256,1024]{1,0:T(8,128)(2,1)} %param.16) | copy-start | bytes 1572868
  11.3 41.3 %copy-start.27 = (f32[1024]{0:T(1024)S(1)}, f32[1024]{0:T(1024)}, u32[]{:S(2)}) copy-start(f32[1024]{0:T(1024)} %param.18) | copy-start | bytes 12292
  12.6 40.2 %collective-permute-start.2 = (bf16[256,1024]{1,0:T(8,128)(2,1)S(1)}, bf16[256,1024]{1,0:T(8,128)(2,1)S(1)}, u32[]{:S(2)}, u32[]{:S(2)}) collective-permute-start(bf16[256,1024]{1,0:T(8,128)(2,1)S(1)} %fusion.146), channel_id=1, source_target_pairs={{0,3},{1,0},{2,1},{3,2},{4,7},{5,4},{6,5},{7,6},{8,11},{9,8},{10,9... | collective-permute-start | bytes 1572872 | tf_op jit(solution)/shard_map/ppermute | solution.py:23
  13.1 26.5 %collective-permute-start = (bf16[256,1024]{1,0:T(8,128)(2,1)S(1)}, bf16[256,1024]{1,0:T(8,128)(2,1)S(1)}, u32[]{:S(2)}, u32[]{:S(2)}) collective-permute-start(bf16[256,1024]{1,0:T(8,128)(2,1)S(1)} %fusion.146), channel_id=1, source_target_pairs={{0,1},{1,2},{2,3},{3,0},{4,5},{5,6},{6,7},{7,4},{8,9},{9,10},{10,1... | collective-permute-start | bytes 1572872 | tf_op jit(solution)/shard_map/ppermute | solution.py:21
  14.7 304.0 %reduce-scatter.20.cloned.1.call-start = ((), (), s32[]{:S(2)}) async-start(), calls=%async_computation.15 | async-start | bytes 589824 | tf_op jit(solution)/shard_map/reduce_scatter | solution.py:208
  24.7 28.5 %copy-start.16 = (bf16[1024,256]{1,0:T(8,128)(2,1)}, bf16[1024,256]{1,0:T(8,128)(2,1)S(1)}, u32[]{:S(2)}) copy-start(bf16[1024,256]{1,0:T(8,128)(2,1)S(1)} %all_gather.20) | copy-start | bytes 1572868
  25.2 28.7 %copy-start.53 = (f32[1,256]{1,0:T(1,128)}, f32[1,256]{1,0:T(1,128)S(1)}, u32[]{:S(2)}) copy-start(f32[1,256]{1,0:T(1,128)S(1)} %get-tuple-element.831) | copy-start | bytes 3076
  25.3 28.7 %copy-start.55 = (f32[1,256]{1,0:T(1,128)}, f32[1,256]{1,0:T(1,128)S(1)}, u32[]{:S(2)}) copy-start(f32[1,256]{1,0:T(1,128)S(1)} %get-tuple-element.832) | copy-start | bytes 3076
  25.3 28.7 %copy-start.57 = (f32[1,256]{1,0:T(1,128)}, f32[1,256]{1,0:T(1,128)S(1)}, u32[]{:S(2)}) copy-start(f32[1,256]{1,0:T(1,128)S(1)} %get-tuple-element.833) | copy-start | bytes 3076
  25.3 28.7 %copy-start.59 = (f32[1,256]{1,0:T(1,128)}, f32[1,256]{1,0:T(1,128)S(1)}, u32[]{:S(2)}) copy-start(f32[1,256]{1,0:T(1,128)S(1)} %get-tuple-element.834) | copy-start | bytes 3076
  39.7 12.8 %collective-permute-start.1 = (bf16[256,1024]{1,0:T(8,128)(2,1)S(1)}, bf16[256,1024]{1,0:T(8,128)(2,1)S(1)}, u32[]{:S(2)}, u32[]{:S(2)}) collective-permute-start(bf16[256,1024]{1,0:T(8,128)(2,1)S(1)} %collective-permute-done), channel_id=1, source_target_pairs={{0,1},{1,2},{2,3},{3,0},{4,5},{5,6},{6,7},{7,4},{8,9},{9,10},{10,1... | collective-permute-start | bytes 1572872 | tf_op jit(solution)/shard_map/ppermute | solution.py:21
  40.3 21.1 %copy-start.40 = (f32[1,512]{1,0:T(1,128)}, f32[1,512]{1,0:T(1,128)S(1)}, u32[]{:S(2)}) copy-start(f32[1,512]{1,0:T(1,128)S(1)} %get-tuple-element.826) | copy-start | bytes 6148
  40.3 21.1 %copy-start.42 = (f32[1,512]{1,0:T(1,128)}, f32[1,512]{1,0:T(1,128)S(1)}, u32[]{:S(2)}) copy-start(f32[1,512]{1,0:T(1,128)S(1)} %get-tuple-element.827) | copy-start | bytes 6148
  40.3 21.1 %copy-start.44 = (f32[1,512]{1,0:T(1,128)}, f32[1,512]{1,0:T(1,128)S(1)}, u32[]{:S(2)}) copy-start(f32[1,512]{1,0:T(1,128)S(1)} %get-tuple-element.828) | copy-start | bytes 6148
  40.3 21.1 %copy-start.46 = (f32[1,512]{1,0:T(1,128)}, f32[1,512]{1,0:T(1,128)S(1)}, u32[]{:S(2)}) copy-start(f32[1,512]{1,0:T(1,128)S(1)} %get-tuple-element.829) | copy-start | bytes 6148
  64.1 94.9 %copy-start.2 = (f32[1,1024,512]{2,1,0:T(8,128)}, f32[1,1024,512]{2,1,0:T(8,128)S(1)}, u32[]{:S(2)}) copy-start(f32[1,1024,512]{2,1,0:T(8,128)S(1)} %get-tuple-element.802) | copy-start | bytes 6291460
  127.5 16.9 %copy-start.62 = (f32[512]{0:T(512)S(1)}, f32[512]{0:T(512)}, u32[]{:S(2)}) copy-start(f32[512]{0:T(512)} %param.26) | copy-start | bytes 6148
  144.3 14.6 %copy-start.32 = (f32[1024]{0:T(1024)}, f32[1024]{0:T(1024)S(1)}, u32[]{:S(2)}) copy-start(f32[1024]{0:T(1024)S(1)} %get-tuple-element.836) | copy-start | bytes 12292
  144.3 14.6 %copy-start.34 = (f32[1024]{0:T(1024)}, f32[1024]{0:T(1024)S(1)}, u32[]{:S(2)}) copy-start(f32[1024]{0:T(1024)S(1)} %get-tuple-element.835) | copy-start | bytes 12292
  176.3 102.2 %copy-start.6 = (f32[1024,256]{1,0:T(8,128)S(1)}, f32[1024,256]{1,0:T(8,128)}, u32[]{:S(2)}) copy-start(f32[1024,256]{1,0:T(8,128)} %copy-done.5) | copy-start | bytes 3145732
  188.6 8.0 %copy-start.50 = (f32[8]{0:T(128)S(1)}, f32[8]{0:T(128)}, u32[]{:S(2)}) copy-start(f32[8]{0:T(128)} %get-tuple-element.1106) | copy-start | bytes 100 | tf_op jit(solution)/shard_map/transpose(jvp(vmap()))/while
  214.3 8.0 %copy-start.50 = (f32[8]{0:T(128)S(1)}, f32[8]{0:T(128)}, u32[]{:S(2)}) copy-start(f32[8]{0:T(128)} %get-tuple-element.1106) | copy-start | bytes 100 | tf_op jit(solution)/shard_map/transpose(jvp(vmap()))/while
  240.0 8.0 %copy-start.50 = (f32[8]{0:T(128)S(1)}, f32[8]{0:T(128)}, u32[]{:S(2)}) copy-start(f32[8]{0:T(128)} %get-tuple-element.1106) | copy-start | bytes 100 | tf_op jit(solution)/shard_map/transpose(jvp(vmap()))/while
  265.8 8.0 %copy-start.50 = (f32[8]{0:T(128)S(1)}, f32[8]{0:T(128)}, u32[]{:S(2)}) copy-start(f32[8]{0:T(128)} %get-tuple-element.1106) | copy-start | bytes 100 | tf_op jit(solution)/shard_map/transpose(jvp(vmap()))/while
  285.1 33.7 %copy-start.8 = (f32[1024,512]{1,0:T(8,128)S(1)}, f32[1024,512]{1,0:T(8,128)}, u32[]{:S(2)}) copy-start(f32[1024,512]{1,0:T(8,128)} %get-tuple-element.798) | copy-start | bytes 6291460
  285.1 33.7 %copy-start.33 = (f32[1024]{0:T(1024)S(1)}, f32[1024]{0:T(1024)}, u32[]{:S(2)}) copy-start(f32[1024]{0:T(1024)} %copy-done.32) | copy-start | bytes 12292
  285.1 33.7 %copy-start.63 = (f32[512]{0:T(512)S(1)}, f32[512]{0:T(512)}, u32[]{:S(2)}) copy-start(f32[512]{0:T(512)} %param.26) | copy-start | bytes 6148
  285.2 79.8 %reduce-scatter.22.cloned.1.call-start = ((), (), s32[]{:S(2)}) async-start(), calls=%async_computation.17 | async-start | bytes 294912
  288.4 104.2 %all-reduce.30.cloned.1.call-start = ((), (), s32[]{:S(2)}) async-start(), calls=%async_computation.16 | async-start | bytes 131072 | tf_op jit(solution)/shard_map/psum | solution.py:218
  318.8 113.0 %reduce-scatter.24.cloned.1.call-start = ((), (), s32[]{:S(2)}) async-start(), calls=%async_computation.18 | async-start | bytes 1179648
  325.3 146.6 %reduce-scatter.16.cloned.1.call-start = ((), (), s32[]{:S(2)}) async-start(), calls=%async_computation.13 | async-start | bytes 1179648 | tf_op jit(solution)/shard_map/reduce_scatter | solution.py:202
  341.1 170.2 %reduce-scatter.18.cloned.1.call-start = ((), (), s32[]{:S(2)}) async-start(), calls=%async_computation.14 | async-start | bytes 1179648 | tf_op jit(solution)/shard_map/reduce_scatter | solution.py:205
  350.8 204.6 %reduce-scatter.14.cloned.1.call-start = ((), (), s32[]{:S(2)}) async-start(), calls=%async_computation.12 | async-start | bytes 2621440 | tf_op jit(solution)/shard_map/reduce_scatter | solution.py:188
  357.4 248.9 %reduce-scatter.12.cloned.1.call-start = ((), (), s32[]{:S(2)}) async-start(), calls=%async_computation.10 | async-start | bytes 2621440 | tf_op jit(solution)/shard_map/reduce_scatter | solution.py:169
  362.8 192.5 %copy-start.28 = (f32[1024]{0:T(1024)S(1)}, f32[1024]{0:T(1024)}, u32[]{:S(2)}) copy-start(f32[1024]{0:T(1024)} %param.18) | copy-start | bytes 12292
  362.8 192.5 %copy-start.39 = (f32[256]{0:T(256)S(1)}, f32[256]{0:T(256)}, u32[]{:S(2)}) copy-start(f32[256]{0:T(256)} %copy-done.38) | copy-start | bytes 3076
  362.8 243.5 %copy-start.15 = (bf16[256,1024]{1,0:T(8,128)(2,1)S(1)}, bf16[256,1024]{1,0:T(8,128)(2,1)}, u32[]{:S(2)}) copy-start(bf16[256,1024]{1,0:T(8,128)(2,1)} %param.17) | copy-start | bytes 1572868
  362.8 243.5 %copy-start.66 = (f32[256]{0:T(256)S(1)}, f32[256]{0:T(256)}, u32[]{:S(2)}) copy-start(f32[256]{0:T(256)} %get-tuple-element.840) | copy-start | bytes 3076
  (65 other events, 230.8 us)
Sparse Core Ops, SparseCore 0:
  10.0 25.1 all-gather.4
  37.1 23.4 all-gather.6
  62.5 23.7 all-gather.8
  87.7 44.3 all-gather.10
  285.3 33.4 reduce-scatter.19
  322.5 33.6 reduce-scatter.21
  358.5 33.9 all-reduce.29
  396.0 35.7 reduce-scatter.23
  435.9 35.9 reduce-scatter.15
  475.3 35.9 reduce-scatter.17
  513.7 41.5 reduce-scatter.13
  557.5 45.3 reduce-scatter.11
